TPU v7x, 32 devices: a whole 2x2x4 slice. The times are simulated.
32 devices in a mesh: row: 4 (over z), col: 4 (over y, x), depth: 2 (over core).
Axes of the slice: x: 2, y: 2, z: 4, core: 2. Of those that a mesh axis runs over, the one named last changes fastest.
Arguments:
- right_sides: float32 [24, 32, 128], P('row'), may hold values from -6 to 6
- factor: float32 [24, 24, 128, 128], P('row', ('col', 'depth')), may hold values from -0.21875 to 0.21875
- pattern: int32 [24, 24], P('row', ('col', 'depth')), may hold values 0 or 1
- inverses: float32 [24, 4, 128, 128], P('row'), may hold values from -0.3 to 2.3, as said below
- supernodes: int32 [24], replicated, may hold values from 0 to 8, never falling along the last dimension, each value on 1 to 4 neighbouring positions
- levels: int32 [9], replicated, may hold values from 0 to 2
Outputs:
- solution: float32 [24, 32, 128], P('row')
Inputs may be any that keep to these rules, and one draw needn't show every extreme that they name: `inverses`: the tile (p, p) has a diagonal of 0.2 to 2.3. `supernodes`: supernode numbers never fall along the tiles; each supernode holds 1 to 4 consecutive tiles.
All inputs are finite; a program needn't handle non-finite values. No bound on the sum of `pattern` on one device may be relied on, other than what follows from the above.
Results may differ from a plain program's by a relative error of at most 0.0001.
Values sent between devices are 32-bit elements; how exact they have to be, the bound alone decides.
A program may use at most 64 MiB of HBM per device.

v0:
```python
import jax
import jax.numpy as jnp
from jax import lax
from jax.sharding import PartitionSpec as P

LEVELS = 3


PREC = lax.Precision.HIGHEST


def from_behind(shard, axis, by):
    size = lax.axis_size(axis)
    pairs = [(i, i + by) for i in range(size) if 0 <= i + by < size]
    return lax.ppermute(shard, axis, pairs)


def spread_2(shard, axis, root):
    mine = lax.axis_index(axis) == root
    return lax.psum(jnp.where(mine, shard, jnp.zeros_like(shard)), axis)


def lookup(values_table, positions):
    slots = lax.broadcasted_iota(jnp.int32, positions.shape + values_table.shape, positions.ndim)
    picked = jnp.where(positions[..., None] == slots, values_table, 0)
    return jnp.sum(picked, axis=-1)


def inverse_band(inverses, supernodes, first_tile):
    tile_count, band_tiles, width = (inverses.shape[0], inverses.shape[1], inverses.shape[2])
    row_index = first_tile + lax.broadcasted_iota(jnp.int32, (tile_count, band_tiles), 0)
    source = (
        row_index - (band_tiles - 1) + lax.broadcasted_iota(jnp.int32, (tile_count, band_tiles), 1)
    )
    clipped = jnp.clip(source, 0, supernodes.shape[0] - 1)
    same_node = (source >= 0) & (lookup(supernodes, clipped) == lookup(supernodes, row_index))
    lower_tri = lax.broadcasted_iota(jnp.int32, (width, width), 0) >= lax.broadcasted_iota(
        jnp.int32, (width, width), 1
    )
    last_tile = lax.broadcasted_iota(jnp.int32, (band_tiles,), 0) == band_tiles - 1
    inner_mask = jnp.where(last_tile[:, None, None], lower_tri[None], True)
    keep_mask = same_node[:, :, None, None] & inner_mask[None]
    return jnp.where(keep_mask, inverses, 0.0)


def apply_lower(diag_band, padded, tile_count):
    band_tiles = diag_band.shape[1]
    windows = jnp.stack(
        [padded[offset : offset + tile_count] for offset in range(band_tiles)], axis=1
    )
    return jnp.einsum("pkij,pkrj->pri", diag_band, windows, precision=PREC)


def apply_upper(diag_band, values):
    band_tiles = diag_band.shape[1]
    contrib = jnp.einsum("pkij,pri->pkrj", diag_band, values, precision=PREC)
    pieces = [
        jnp.pad(contrib[:, offset], ((offset, band_tiles - 1 - offset), (0, 0), (0, 0)))
        for offset in range(band_tiles)
    ]
    return sum(pieces)


def shards(right_sides, factor, pattern, inverses, supernodes, levels):
    row_tiles = right_sides.shape[0]
    col_tiles = factor.shape[1]
    rim_tiles = inverses.shape[1] - 1
    row_first = lax.axis_index("row") * row_tiles
    col_first = (
        lax.axis_index("col") * lax.axis_size("depth") + lax.axis_index("depth")
    ) * col_tiles
    tile_level = lookup(levels, supernodes)
    row_level = lax.dynamic_slice_in_dim(tile_level, row_first, row_tiles)
    col_level = lax.dynamic_slice_in_dim(tile_level, col_first, col_tiles)
    keep_mask = (row_level[:, None] > col_level[None, :]) & (pattern > 0)
    masked = jnp.where(keep_mask[:, :, None, None], factor, 0.0)
    diag_band = inverse_band(inverses, supernodes, row_first)
    solved = jnp.zeros_like(right_sides)
    columns = jnp.zeros((col_tiles,) + right_sides.shape[1:], jnp.float32)
    for level_now in range(LEVELS):
        if level_now > 0:
            partial_sum = jnp.einsum("pqij,qrj->pri", masked, columns, precision=PREC)
            residual = right_sides - lax.psum(partial_sum, ("col", "depth"))
        else:
            residual = right_sides
        before = from_behind(residual[row_tiles - rim_tiles :], "row", 1)
        update = apply_lower(diag_band, jnp.concatenate([before, residual], 0), row_tiles)
        solved = jnp.where((row_level == level_now)[:, None, None], update, solved)
        if level_now + 1 < LEVELS:
            spread = spread_2(solved, "row", lax.axis_index("col"))
            columns = lax.dynamic_slice_in_dim(
                spread, lax.axis_index("depth") * col_tiles, col_tiles, 0
            )
    answer = jnp.zeros_like(right_sides)
    for level_now in range(LEVELS - 1, -1, -1):
        if level_now < LEVELS - 1:
            partial_sum = jnp.einsum("pqij,pri->qrj", masked, answer, precision=PREC)
            column_sum = lax.psum(partial_sum, "row")
            gathered = lax.all_gather(column_sum, ("col", "depth"), axis=0, tiled=True)
            row_sum = lax.dynamic_slice_in_dim(gathered, row_first, row_tiles, 0)
            residual = solved - row_sum
        else:
            residual = solved
        padded = apply_upper(diag_band, residual)
        from_next = from_behind(padded[:rim_tiles], "row", -1)
        update = padded[rim_tiles:] + jnp.concatenate(
            [jnp.zeros_like(padded[: row_tiles - rim_tiles]), from_next], 0
        )
        answer = jnp.where((row_level == level_now)[:, None, None], update, answer)
    return answer


def solution(mesh):
    return jax.shard_map(
        shards,
        mesh=mesh,
        in_specs=(
            P("row", None, None),
            P("row", ("col", "depth"), None, None),
            P("row", ("col", "depth")),
            P("row", None, None, None),
            P(),
            P(),
        ),
        out_specs=P("row", None, None),
        check_vma=False,
    )
```

profile of v0, /device:TPU:0, one launch (start us, length us, event | category | flops | bytes accessed | tf_op | source)
XLA Modules:
  0.0 300.8 jit_solution(13699101733195636206)
XLA Ops:
  7.3 4.9 %collective-permute-start = (f32[3,32,128]{2,1,0:T(8,128)S(1)}, f32[3,32,128]{2,1,0:T(8,128)S(1)}, u32[]{:S(2)}, u32[]{:S(2)}) collective-permute-start(f32[3,32,128]{2,1,0:T(8,128)S(1)} %slice.90), channel_id=1, source_target_pairs={{0,8},{8,16},{16,24},{1,9},{9,17},{17,25},{2,10},{10,18},{18,26},{... | collective-permute-start | bytes 147464 | tf_op jit(solution)/shard_map/ppermute | solution.py:15
  15.6 3.9 %broadcast_select_fusion.2 = (f32[6,32,128]{2,1,0:T(8,128)}, f32[6,32,128]{2,1,0:T(8,128)S(1)}) fusion(pred[]{:T(512)S(6)} %eq.58, f32[6,1,32,128]{3,2,1,0:T(8,128)} %bitcast.118, f32[6,1,32,128]{3,2,1,0:T(8,128)S(1)} %get-tuple-element.28, f32[6,1,32,128]{3,2,1,0:T(8,128)S(1)} %get-tuple-element.29, f32[6,1,32,128]{3,2,1,0:T(8,128)S(1)} %get-tuple-element.27, ...), kind=kOutput, calls=%fused_computation.118 | convolution fusion | flops 152125440 | bytes 2228255 | tf_op jit(solution)/shard_map/pkij,pkrj->pri/dot_general | solution.py:51
  19.8 35.6 %all-reduce.20.cloned.1.call-done = f32[6,32,128]{2,1,0:T(8,128)} async-done(((f32[6,32,128]{2,1,0:T(8,128)}), f32[6,32,128]{2,1,0:T(8,128)}) %all-reduce.20.cloned.1.call-update) | async-done | bytes 98320 | tf_op jit(solution)/shard_map/psum | solution.py:20
  55.4 2.7 convolution_bitcast_fusion.4
  58.2 51.8 %all-reduce.22.cloned.1.call-done = f32[6,32,128]{2,1,0:T(8,128)} async-done(((f32[6,32,128]{2,1,0:T(8,128)}), f32[6,32,128]{2,1,0:T(8,128)}) %all-reduce.22.cloned.1.call-update) | async-done | bytes 98320 | tf_op jit(solution)/shard_map/psum | solution.py:83
  110.9 3.4 %collective-permute-start.1 = (f32[3,32,128]{2,1,0:T(8,128)S(1)}, f32[3,32,128]{2,1,0:T(8,128)S(1)}, u32[]{:S(2)}, u32[]{:S(2)}) collective-permute-start(f32[3,32,128]{2,1,0:T(8,128)S(1)} %slice.123), channel_id=1, source_target_pairs={{0,8},{8,16},{16,24},{1,9},{9,17},{17,25},{2,10},{10,18},{18,26},{... | collective-permute-start | bytes 147464 | tf_op jit(solution)/shard_map/ppermute | solution.py:15
  114.3 1.7 collective-permute-done.1
  116.1 2.4 broadcast_select_fusion.1
  118.6 36.0 %all-reduce.24.cloned.1.call-done = f32[6,32,128]{2,1,0:T(8,128)} async-done(((f32[6,32,128]{2,1,0:T(8,128)}), f32[6,32,128]{2,1,0:T(8,128)}) %all-reduce.24.cloned.1.call-update) | async-done | bytes 98320 | tf_op jit(solution)/shard_map/psum | solution.py:20
  154.6 2.7 convolution_bitcast_fusion.3
  157.3 51.7 %all-reduce.26.cloned.1.call-done = f32[6,32,128]{2,1,0:T(8,128)} async-done(((f32[6,32,128]{2,1,0:T(8,128)}), f32[6,32,128]{2,1,0:T(8,128)}) %all-reduce.26.cloned.1.call-update) | async-done | bytes 98320 | tf_op jit(solution)/shard_map/psum | solution.py:83
  209.9 3.4 %collective-permute-start.2 = (f32[3,32,128]{2,1,0:T(8,128)S(1)}, f32[3,32,128]{2,1,0:T(8,128)S(1)}, u32[]{:S(2)}, u32[]{:S(2)}) collective-permute-start(f32[3,32,128]{2,1,0:T(8,128)S(1)} %slice.128), channel_id=1, source_target_pairs={{0,8},{8,16},{16,24},{1,9},{9,17},{17,25},{2,10},{10,18},{18,26},{... | collective-permute-start | bytes 147464 | tf_op jit(solution)/shard_map/ppermute | solution.py:15
  213.3 1.7 collective-permute-done.2
  215.1 1.8 fusion.14
  218.0 1.3 collective-permute-start.3
  219.4 5.0 %collective-permute-done.3 = f32[3,32,128]{2,1,0:T(8,128)S(1)} collective-permute-done((f32[3,32,128]{2,1,0:T(8,128)S(1)}, f32[3,32,128]{2,1,0:T(8,128)S(1)}, u32[]{:S(2)}, u32[]{:S(2)}) %collective-permute-start.3) | collective-permute-done | bytes 49184 | tf_op jit(solution)/shard_map/ppermute | solution.py:15
  225.2 18.1 %psum.46 = f32[3,32,128]{2,1,0:T(8,128)S(1)} all-reduce(f32[3,32,128]{2,1,0:T(8,128)S(1)} %convolution_bitcast_fusion.7), channel_id=1, replica_groups=mesh['row'=4,'col'=4,'depth'=2] {'row'}, use_global_device_ids=true, to_apply=%region_7.8 | all-reduce | flops 12288 | bytes 98304 | tf_op jit(solution)/shard_map/psum | solution.py:98
  243.3 10.4 %all_gather.6 = f32[24,32,128]{2,1,0:T(8,128)S(1)} all-gather(f32[3,32,128]{2,1,0:T(8,128)S(1)} %psum.46), channel_id=1, replica_groups=mesh['row'=4,'col'=4,'depth'=2] {'col','depth'}, dimensions={0}, use_global_device_ids=true | all-gather | bytes 442368 | tf_op jit(solution)/shard_map/all_gather | solution.py:99
  254.9 1.3 collective-permute-start.4
  256.2 4.6 %collective-permute-done.4 = f32[3,32,128]{2,1,0:T(8,128)S(1)} collective-permute-done((f32[3,32,128]{2,1,0:T(8,128)S(1)}, f32[3,32,128]{2,1,0:T(8,128)S(1)}, u32[]{:S(2)}, u32[]{:S(2)}) %collective-permute-start.4) | collective-permute-done | bytes 49184 | tf_op jit(solution)/shard_map/ppermute | solution.py:15
  261.7 16.1 %psum.47 = f32[3,32,128]{2,1,0:T(8,128)S(1)} all-reduce(f32[3,32,128]{2,1,0:T(8,128)S(1)} %convolution_bitcast_fusion.6), channel_id=1, replica_groups=mesh['row'=4,'col'=4,'depth'=2] {'row'}, use_global_device_ids=true, to_apply=%region_8.9 | all-reduce | flops 12288 | bytes 98304 | tf_op jit(solution)/shard_map/psum | solution.py:98
  277.8 8.5 %all_gather.7 = f32[24,32,128]{2,1,0:T(8,128)S(1)} all-gather(f32[3,32,128]{2,1,0:T(8,128)S(1)} %psum.47), channel_id=1, replica_groups=mesh['row'=4,'col'=4,'depth'=2] {'col','depth'}, dimensions={0}, use_global_device_ids=true | all-gather | bytes 442368 | tf_op jit(solution)/shard_map/all_gather | solution.py:99
  287.6 1.3 collective-permute-start.5
  288.9 4.6 %collective-permute-done.5 = f32[3,32,128]{2,1,0:T(8,128)S(1)} collective-permute-done((f32[3,32,128]{2,1,0:T(8,128)S(1)}, f32[3,32,128]{2,1,0:T(8,128)S(1)}, u32[]{:S(2)}, u32[]{:S(2)}) %collective-permute-start.5) | collective-permute-done | bytes 49184 | tf_op jit(solution)/shard_map/ppermute | solution.py:15
  (56 shorter events, 12.3 us)
Async XLA Ops:
  6.5 48.9 %all-reduce.20.cloned.1.call-start = ((), (), s32[]{:S(2)}) async-start(), calls=%async_computation | async-start | bytes 196608 | tf_op jit(solution)/shard_map/psum | solution.py:20
  7.3 7.2 %collective-permute-start = (f32[3,32,128]{2,1,0:T(8,128)S(1)}, f32[3,32,128]{2,1,0:T(8,128)S(1)}, u32[]{:S(2)}, u32[]{:S(2)}) collective-permute-start(f32[3,32,128]{2,1,0:T(8,128)S(1)} %slice.90), channel_id=1, source_target_pairs={{0,8},{8,16},{16,24},{1,9},{9,17},{17,25},{2,10},{10,18},{18,26},{... | collective-permute-start | bytes 147464 | tf_op jit(solution)/shard_map/ppermute | solution.py:15
  14.5 5.0 %copy-start.3 = (s32[6,3]{0,1:T(4,128)S(1)}, s32[6,3]{0,1:T(4,128)}, u32[]{:S(2)}) copy-start(s32[6,3]{0,1:T(4,128)} %param.8) | copy-start | bytes 220
  14.5 40.9 %copy-start.1 = (f32[6,3,128,128]{3,2,1,0:T(8,128)S(1)}, f32[6,3,128,128]{3,2,1,0:T(8,128)}, u32[]{:S(2)}) copy-start(f32[6,3,128,128]{3,2,1,0:T(8,128)} %param.7) | copy-start | bytes 3538948
  15.6 94.4 %copy-start.2 = (f32[6,32,128]{2,1,0:T(8,128)S(1)}, f32[6,32,128]{2,1,0:T(8,128)}, u32[]{:S(2)}) copy-start(f32[6,32,128]{2,1,0:T(8,128)} %param.6) | copy-start | bytes 294916
  19.5 96.6 %copy-start = (f32[6,4,128,128]{3,2,1,0:T(8,128)S(1)}, f32[6,4,128,128]{3,2,1,0:T(8,128)}, u32[]{:S(2)}) copy-start(f32[6,4,128,128]{3,2,1,0:T(8,128)} %param.9) | copy-start | bytes 4718596
  19.5 90.5 %all-reduce.22.cloned.1.call-start = ((), (), s32[]{:S(2)}) async-start(), calls=%async_computation.1 | async-start | bytes 196608 | tf_op jit(solution)/shard_map/psum | solution.py:83
  58.1 96.4 %all-reduce.24.cloned.1.call-start = ((), (), s32[]{:S(2)}) async-start(), calls=%async_computation.2 | async-start | bytes 196608 | tf_op jit(solution)/shard_map/psum | solution.py:20
  110.9 5.1 %collective-permute-start.1 = (f32[3,32,128]{2,1,0:T(8,128)S(1)}, f32[3,32,128]{2,1,0:T(8,128)S(1)}, u32[]{:S(2)}, u32[]{:S(2)}) collective-permute-start(f32[3,32,128]{2,1,0:T(8,128)S(1)} %slice.123), channel_id=1, source_target_pairs={{0,8},{8,16},{16,24},{1,9},{9,17},{17,25},{2,10},{10,18},{18,26},{... | collective-permute-start | bytes 147464 | tf_op jit(solution)/shard_map/ppermute | solution.py:15
  118.5 90.5 %all-reduce.26.cloned.1.call-start = ((), (), s32[]{:S(2)}) async-start(), calls=%async_computation.3 | async-start | bytes 196608 | tf_op jit(solution)/shard_map/psum | solution.py:83
  209.9 5.1 %collective-permute-start.2 = (f32[3,32,128]{2,1,0:T(8,128)S(1)}, f32[3,32,128]{2,1,0:T(8,128)S(1)}, u32[]{:S(2)}, u32[]{:S(2)}) collective-permute-start(f32[3,32,128]{2,1,0:T(8,128)S(1)} %slice.128), channel_id=1, source_target_pairs={{0,8},{8,16},{16,24},{1,9},{9,17},{17,25},{2,10},{10,18},{18,26},{... | collective-permute-start | bytes 147464 | tf_op jit(solution)/shard_map/ppermute | solution.py:15
  218.0 6.3 %collective-permute-start.3 = (f32[3,32,128]{2,1,0:T(8,128)S(1)}, f32[3,32,128]{2,1,0:T(8,128)S(1)}, u32[]{:S(2)}, u32[]{:S(2)}) collective-permute-start(f32[3,32,128]{2,1,0:T(8,128)S(1)} %pad_add_fusion.5), channel_id=1, source_target_pairs={{8,0},{16,8},{24,16},{9,1},{17,9},{25,17},{10,2},{18,10},{26,18},{... | collective-permute-start | bytes 147464 | tf_op jit(solution)/shard_map/ppermute | solution.py:15
  254.9 6.0 %collective-permute-start.4 = (f32[3,32,128]{2,1,0:T(8,128)S(1)}, f32[3,32,128]{2,1,0:T(8,128)S(1)}, u32[]{:S(2)}, u32[]{:S(2)}) collective-permute-start(f32[3,32,128]{2,1,0:T(8,128)S(1)} %pad_add_fusion.4), channel_id=1, source_target_pairs={{8,0},{16,8},{24,16},{9,1},{17,9},{25,17},{10,2},{18,10},{26,18},{... | collective-permute-start | bytes 147464 | tf_op jit(solution)/shard_map/ppermute | solution.py:15
  287.6 6.0 %collective-permute-start.5 = (f32[3,32,128]{2,1,0:T(8,128)S(1)}, f32[3,32,128]{2,1,0:T(8,128)S(1)}, u32[]{:S(2)}, u32[]{:S(2)}) collective-permute-start(f32[3,32,128]{2,1,0:T(8,128)S(1)} %pad_add_fusion.3), channel_id=1, source_target_pairs={{8,0},{16,8},{24,16},{9,1},{17,9},{25,17},{10,2},{18,10},{26,18},{... | collective-permute-start | bytes 147464 | tf_op jit(solution)/shard_map/ppermute | solution.py:15
Sparse Core Ops, SparseCore 0:
  19.6 35.7 all-reduce.19
  58.8 51.1 all-reduce.21
  118.6 35.8 all-reduce.23
  157.8 51.1 all-reduce.25
where the time goes:
time: 301 us
  waiting for transfers between devices  193 us (64%)
  blocking collectives  53.1 us (18%)
  matrix products  18.4 us (6%)
  starting transfers between devices  15.7 us (5%)
  between operations  13.5 us (4%)
  other arithmetic  4.98 us (2%)
    psum x2, waiting for transfers between devices, shards(): residual = right_sides - lax.psum(partial_sum, ('col', 'depth'))  104 us
    psum x2, waiting for transfers between devices, spread_2(): return lax.psum(jnp.where(mine, shard, jnp.zeros_like(shard)), axis)  71.6 us
    psum x2, blocking collectives, shards(): column_sum = lax.psum(partial_sum, 'row')  34.2 us
    all_gather x2, blocking collectives, shards(): gathered = lax.all_gather(column_sum, ('col', 'depth'), axis=0, tiled=True)  18.9 us
    ppermute x6, waiting for transfers between devices, from_behind(): return lax.ppermute(shard, axis, pairs)  17.7 us
    ppermute x6, starting transfers between devices, from_behind(): return lax.ppermute(shard, axis, pairs)  15.6 us
    dot_general x3, matrix products, apply_lower(): return jnp.einsum('pkij,pkrj->pri', diag_band, windows, precision=PREC)  8.07 us
  transfers between devices with their start and end apart: 10, of which 9 were waited for; matrix products, arithmetic and copies ran while one was open for 1% of the time, Pallas kernels for 0%

commit v1 on v0

v1 whole, which is shorter than its diff:
```python
import functools

import jax
import jax.numpy as jnp
from jax import lax
from jax.experimental import pallas as pl
from jax.experimental.pallas import tpu as pltpu
from jax.sharding import PartitionSpec as P

LEVELS = 3
MESH = pl.DeviceIdType.MESH
F32, BF16 = jnp.float32, jnp.bfloat16
ROWS_BY_ROWS = (((1,), (1,)), ((), ()))
ROWS_BY_COLS = (((1,), (0,)), ((), ()))


def halves(x):
    high = x.astype(BF16).astype(F32)
    return high, x - high


def product(x, w_high, w_low, dims):
    count = x.shape[0]
    stacked = jnp.concatenate(halves(x), axis=0).astype(BF16)
    both = lax.dot_general(stacked, w_high, dims, preferred_element_type=F32)
    both += lax.dot_general(stacked, w_low, dims, preferred_element_type=F32)
    return both[:count] + both[count:]


def kernel(
    rows, cols, depths, rhs_ref, factor_hbm, pattern_ref, inverses_hbm, supernodes_ref, levels_ref,
    out_ref,
    factor_ref, inverses_ref, w_high, w_low, d_high, d_low,
    start_ref, wide_ref, pad_ref, solved_ref, answer_ref,
    send_d, recv_d, send_b, recv_b, send_e, recv_e, send_g, recv_g,
    load_sems, start_sems, d_sems, b_sems, e_sems, g_sems,
):
    row, col, depth = lax.axis_index("row"), lax.axis_index("col"), lax.axis_index("depth")
    group = cols * depths
    place = col * depths + depth
    row_tiles, rhs, width = rhs_ref.shape
    col_tiles = factor_ref.shape[1]
    band = inverses_ref.shape[1]
    chunk = rhs // cols
    span = col_tiles * width
    first, last = row == 0, row == rows - 1
    upper, lower = depth == 1, depth == 0
    home = row == col

    def device(to_row, to_col, to_depth):
        return {"row": to_row, "col": to_col, "depth": to_depth}

    barrier = pltpu.get_barrier_semaphore()
    count = rows * group
    me = row * group + place

    def greet(i, carry):
        to = lax.rem(me + i, count)
        to_place = lax.rem(to, group)
        pl.semaphore_signal(
            barrier, inc=1,
            device_id=device(to // group, to_place // depths, lax.rem(to_place, depths)),
            device_id_type=MESH,
        )
        return carry

    load_inverses = pltpu.make_async_copy(
        inverses_hbm.at[pl.ds(depth * col_tiles, col_tiles)], inverses_ref, load_sems.at[0]
    )
    load_factor = pltpu.make_async_copy(factor_hbm, factor_ref, load_sems.at[1])
    load_inverses.start()
    load_factor.start()
    lax.fori_loop(1, count, greet, 0, unroll=count <= 64)

    def push(src, dst, sems, to):
        pltpu.make_async_remote_copy(
            src_ref=src, dst_ref=dst, send_sem=sems.at[0], recv_sem=sems.at[1],
            device_id=to, device_id_type=MESH,
        ).start()

    def await_units(ruler, sem, cases):
        for condition, units in cases:
            if units:

                @pl.when(condition)
                def _(units=units):
                    part = ruler.at[pl.ds(0, units)]
                    pltpu.make_async_copy(part, part, sem).wait()

    def level_of(tile):
        return levels_ref[supernodes_ref[tile]]

    def lanes(scalars):
        return jnp.concatenate([jnp.full((1, width), s, F32) for s in scalars], axis=1)

    one, zero = jnp.float32(1), jnp.float32(0)

    for p in range(row_tiles):
        half, t = divmod(p, col_tiles)
        piece = rhs_ref[p, pl.ds(pl.multiple_of(col * chunk, chunk), chunk), :]

        @pl.when(depth == half)
        def _(t=t, piece=piece):
            start_ref[1, :, t * width : (t + 1) * width] = piece

        if half == 0:

            @pl.when(upper)
            def _(t=t, piece=piece):
                start_ref[0, :, t * width : (t + 1) * width] = piece

    @pl.when(lower & first)
    def _():
        start_ref[0] = jnp.zeros((chunk, span), F32)

    pl.semaphore_wait(barrier, count - 1)

    @pl.when(upper & jnp.logical_not(last))
    def _():
        push(start_ref.at[1], start_ref.at[0], start_sems, device(row + 1, col, 0))

    load_inverses.wait()
    own_first = row * row_tiles + depth * col_tiles
    own_level = [level_of(own_first + t) for t in range(col_tiles)]
    under = lax.broadcasted_iota(jnp.int32, (width, width), 0) >= lax.broadcasted_iota(
        jnp.int32, (width, width), 1
    )
    for t in range(col_tiles):
        tile = own_first + t
        for k in range(band):
            source = tile - (band - 1) + k
            if k == band - 1:
                kept = jnp.where(under, inverses_ref[t, k], 0.0)
            else:
                same = (source >= 0) & (
                    supernodes_ref[jnp.maximum(source, 0)] == supernodes_ref[tile]
                )
                kept = inverses_ref[t, k] * jnp.where(same, one, zero)
            high, low = halves(kept)
            d_high[t, :, k * width : (k + 1) * width] = high.astype(BF16)
            d_low[t, :, k * width : (k + 1) * width] = low.astype(BF16)

    @pl.when(lower & jnp.logical_not(first))
    def _():
        pltpu.make_async_copy(start_ref.at[0], start_ref.at[0], start_sems.at[1]).wait()

    own_mask = [
        lanes([jnp.where(v == level, one, zero) for v in own_level]) for level in range(LEVELS)
    ]

    def widen(value):
        if chunk >= 8:
            return value
        pad_ref[...] = jnp.zeros_like(pad_ref)
        pad_ref[0:chunk, 0 : value.shape[1]] = value
        return pad_ref[:, 0 : value.shape[1]]

    def solve_own(level, residual):
        x = widen(residual)
        update = jnp.concatenate(
            [
                product(
                    x[:, t * width : (t + band) * width], d_high[t], d_low[t], ROWS_BY_ROWS
                )
                for t in range(col_tiles)
            ],
            axis=1,
        )[:chunk]
        now = update * own_mask[level]
        solved_ref[...] = now if level == 0 else solved_ref[...] + now

    def spread_solved(level):
        send_d[level] = solved_ref[...]
        for to in range(rows):

            @pl.when(jnp.logical_not(home & (row == to)))
            def _(to=to):
                push(send_d.at[level], recv_d.at[level, col], d_sems.at[level], device(to, row, depth))

        @pl.when(home)
        def _():
            recv_d[level, col] = solved_ref[...]

    def start_vector():
        return jnp.concatenate([start_ref[0], start_ref[1]], axis=1)

    solve_own(0, start_vector())
    spread_solved(0)

    load_factor.wait()
    row_level = [level_of(row * row_tiles + p) for p in range(row_tiles)]
    col_level = [level_of(place * col_tiles + q) for q in range(col_tiles)]
    for p in range(row_tiles):
        for q in range(col_tiles):
            keep = (row_level[p] > col_level[q]) & (pattern_ref[p, q] > 0)
            high, low = halves(factor_ref[p, q] * jnp.where(keep, one, zero))
            at = (slice(p * width, (p + 1) * width), slice(q * width, (q + 1) * width))
            w_high[at] = high.astype(BF16)
            w_low[at] = low.astype(BF16)
    row_mask = [
        lanes([jnp.where(v == level, one, zero) for v in row_level]) for level in range(LEVELS)
    ]

    column_cases = [(jnp.logical_not(home), rows), (home, rows - 1)]

    def reduce_rows(level):
        await_units(recv_d.at[level], d_sems.at[level, 1], column_cases)
        for k in range(cols):
            wide_ref[k * chunk : (k + 1) * chunk, 0:span] = recv_d[level, k]
        wide_ref[...] = product(wide_ref[:, 0:span], w_high[...], w_low[...], ROWS_BY_ROWS)
        for k in range(cols):
            for half in range(2):
                send_b[level, k, half] = wide_ref[
                    k * chunk : (k + 1) * chunk, half * span : (half + 1) * span
                ]
        src, dst, sems = send_b.at[level], recv_b.at[level], b_sems.at[level]

        for step in range(1, group):
            to = lax.rem(place + step, group)
            to_col, to_depth = to // depths, lax.rem(to, depths)
            slot = group - step

            @pl.when(to_depth == 1)
            def _(to_col=to_col, slot=slot):
                push(
                    src.at[to_col], dst.at[pl.ds(2 * slot, 2)], sems, device(row, to_col, 1)
                )

            @pl.when(to_depth == 0)
            def _(to_col=to_col, slot=slot):
                push(
                    src.at[to_col, 0], dst.at[2 * slot + 1], sems, device(row, to_col, 0)
                )

        @pl.when(jnp.logical_not(last))
        def _():
            for k in range(cols):
                slot = lax.rem(place - k * depths + group, group)
                push(src.at[k, 1], dst.at[2 * slot], sems, device(row + 1, k, 0))

        recv_b[level, 1] = send_b[level, col, depth]

        @pl.when(upper)
        def _():
            recv_b[level, 0] = send_b[level, col, 0]

        @pl.when(lower & first)
        def _():
            for slot in range(group):
                recv_b[level, 2 * slot] = jnp.zeros((chunk, span), F32)

        await_units(
            dst, sems.at[1],
            [
                (upper, 2 * (group - 1)),
                (lower & first, group - 1),
                (lower & jnp.logical_not(first), 2 * group - 1),
            ],
        )
        sums = []
        for part in range(2):
            total = recv_b[level, part]
            for slot in range(1, group):
                total += recv_b[level, 2 * slot + part]
            sums.append(total)
        return jnp.concatenate(sums, axis=1)

    for level in range(1, LEVELS):
        solve_own(level, start_vector() - reduce_rows(level - 1))
        if level + 1 < LEVELS:
            spread_solved(level)

    gather_sends = [
        (upper, 2 * (group - 1)),
        (lower & first, group - 1),
        (lower & jnp.logical_not(first), 2 * group - 1),
    ]
    whole = cols + 2 * cols
    gather_receives = [
        (upper & last, whole - 2),
        (lower & last, whole - 1),
        (upper & jnp.logical_not(last), whole - 2 + cols),
        (lower & jnp.logical_not(last), whole - 1 + cols),
    ]

    def spread_answer(step, residual):
        x = widen(residual)
        pieces = [None] * (2 * col_tiles)
        for t in range(col_tiles):
            given = product(
                x[:, t * width : (t + 1) * width], d_high[t], d_low[t], ROWS_BY_COLS
            )
            for k in range(band):
                piece = given[:chunk, k * width : (k + 1) * width]
                u = t + k - (band - 1) + col_tiles
                pieces[u] = piece if pieces[u] is None else pieces[u] + piece
        for u, piece in enumerate(pieces):
            half, t = divmod(u, col_tiles)
            send_e[step, half, :, t * width : (t + 1) * width] = (
                jnp.zeros((chunk, width), F32) if piece is None else piece
            )
        src, dst, sems = send_e.at[step], recv_e.at[step], e_sems.at[step]

        @pl.when(upper)
        def _():
            for other in range(1, group):
                to = lax.rem(place + other, group)
                push(
                    src, dst.at[pl.ds(2 * col, 2)], sems,
                    device(row, to // depths, lax.rem(to, depths)),
                )
            recv_e[step, pl.ds(2 * col, 2)] = send_e[step]

        @pl.when(lower)
        def _():
            for other in range(1, group):
                to = lax.rem(place + other, group)
                push(
                    src.at[1], dst.at[2 * cols + 2 * col], sems,
                    device(row, to // depths, lax.rem(to, depths)),
                )
            recv_e[step, 2 * cols + 2 * col] = send_e[step, 1]

        @pl.when(lower & jnp.logical_not(first))
        def _():
            for to in range(group):
                push(
                    src.at[0], dst.at[2 * cols + 2 * col + 1], sems,
                    device(row - 1, to // depths, to % depths),
                )

        @pl.when(last)
        def _():
            for k in range(cols):
                recv_e[step, 2 * cols + 2 * k + 1] = jnp.zeros((chunk, span), F32)

        await_units(dst, sems.at[1], gather_receives)
        mask = row_mask[LEVELS - 1 - step]
        for k in range(cols):
            for half in range(2):
                at = (slice(k * chunk, (k + 1) * chunk), slice(half * span, (half + 1) * span))
                now = recv_e[step, 2 * k + half] + recv_e[step, 2 * cols + 2 * k + half]
                now = now * mask[:, half * span : (half + 1) * span]
                answer_ref[at] = now if step == 0 else answer_ref[at] + now

    def column_sums(step):
        wide_ref[:, 0:span] = product(answer_ref[...], w_high[...], w_low[...], ROWS_BY_COLS)
        for k in range(cols):
            send_g[step, k] = wide_ref[k * chunk : (k + 1) * chunk, 0:span]
        for k in range(cols):

            @pl.when(jnp.logical_not(home & (col == k)))
            def _(k=k):
                push(
                    send_g.at[step, k], recv_g.at[step, row], g_sems.at[step], device(col, k, depth)
                )

        @pl.when(home)
        def _():
            recv_g[step, row] = send_g[step, col]

        await_units(recv_g.at[step], g_sems.at[step, 1], column_cases)
        total = recv_g[step, 0]
        for r in range(1, rows):
            total += recv_g[step, r]
        return total

    spread_answer(0, solved_ref[...])
    for step in range(1, LEVELS):
        spread_answer(step, solved_ref[...] - column_sums(step - 1))

    for p in range(row_tiles):
        out_ref[p] = answer_ref[:, p * width : (p + 1) * width]

    @pl.when(upper & jnp.logical_not(last))
    def _():
        pltpu.make_async_copy(start_ref.at[1], start_ref.at[1], start_sems.at[0]).wait()

    reduce_sends = [
        (upper & last, whole - 2),
        (lower & last, whole - 1),
        (upper & jnp.logical_not(last), whole - 2 + cols),
        (lower & jnp.logical_not(last), whole - 1 + cols),
    ]
    for level in range(LEVELS - 1):
        await_units(recv_d.at[level], d_sems.at[level, 0], column_cases)
        await_units(recv_b.at[level], b_sems.at[level, 0], reduce_sends)
        await_units(recv_g.at[level], g_sems.at[level, 0], column_cases)
    for step in range(LEVELS):
        await_units(recv_e.at[step], e_sems.at[step, 0], gather_sends)


def shards(rows, cols, depths, right_sides, factor, pattern, inverses, supernodes, levels):
    row_tiles, rhs, width = right_sides.shape
    col_tiles, band = factor.shape[1], inverses.shape[1]
    group = cols * depths
    assert depths == 2 and rows == cols and row_tiles == depths * col_tiles
    assert rhs % cols == 0 and band - 1 <= col_tiles
    chunk, span = rhs // cols, col_tiles * width
    unit = (chunk, span)
    vmem = pl.BlockSpec(memory_space=pltpu.VMEM)
    smem = pl.BlockSpec(memory_space=pltpu.SMEM)
    hbm = pl.BlockSpec(memory_space=pl.ANY)
    steps = LEVELS - 1
    dma = pltpu.SemaphoreType.DMA
    return pl.pallas_call(
        functools.partial(kernel, rows, cols, depths),
        out_shape=jax.ShapeDtypeStruct(right_sides.shape, F32),
        in_specs=[vmem, hbm, smem, hbm, smem, smem],
        out_specs=vmem,
        scratch_shapes=[
            pltpu.VMEM(factor.shape, F32),
            pltpu.VMEM((col_tiles,) + inverses.shape[1:], F32),
            pltpu.VMEM((row_tiles * width, span), BF16),
            pltpu.VMEM((row_tiles * width, span), BF16),
            pltpu.VMEM((col_tiles, width, band * width), BF16),
            pltpu.VMEM((col_tiles, width, band * width), BF16),
            pltpu.VMEM((2,) + unit, F32),
            pltpu.VMEM((rhs, row_tiles * width), F32),
            pltpu.VMEM((8, row_tiles * width), F32),
            pltpu.VMEM(unit, F32),
            pltpu.VMEM((rhs, row_tiles * width), F32),
            pltpu.VMEM((steps,) + unit, F32),
            pltpu.VMEM((steps, cols) + unit, F32),
            pltpu.VMEM((steps, cols, 2) + unit, F32),
            pltpu.VMEM((steps, 2 * group) + unit, F32),
            pltpu.VMEM((LEVELS, 2) + unit, F32),
            pltpu.VMEM((LEVELS, 4 * cols) + unit, F32),
            pltpu.VMEM((steps, cols) + unit, F32),
            pltpu.VMEM((steps, rows) + unit, F32),
            dma((2,)),
            dma((2,)),
            dma((steps, 2)),
            dma((steps, 2)),
            dma((LEVELS, 2)),
            dma((steps, 2)),
        ],
        compiler_params=pltpu.CompilerParams(
            collective_id=0, has_side_effects=True, vmem_limit_bytes=32 * 1024 * 1024
        ),
    )(right_sides, factor, pattern, inverses, supernodes, levels)


def solution(mesh):
    rows, cols, depths = (mesh.shape[axis] for axis in ("row", "col", "depth"))
    return jax.shard_map(
        functools.partial(shards, rows, cols, depths),
        mesh=mesh,
        in_specs=(
            P("row", None, None),
            P("row", ("col", "depth"), None, None),
            P("row", ("col", "depth")),
            P("row", None, None, None),
            P(),
            P(),
        ),
        out_specs=P("row", None, None),
        check_vma=False,
    )
```

time: 301 us -> 57.5 us (0.19)
  waiting for transfers between devices: 193 us -> 0 us
  blocking collectives: 53.1 us -> 0 us
  Pallas kernels: 0 us -> 50.9 us
  matrix products: 18.4 us -> 0 us
  starting transfers between devices: 15.7 us -> 0 us
  between operations: 13.5 us -> 0.01 us
  other arithmetic: 4.98 us -> 0 us
  local copies, waits for them, and re-layouts: 2.13 us -> 6.29 us
    psum x4 -> x0, waiting for transfers between devices: 175 us -> none  [the longest x2 104 us: shards(): residual = right_sides - lax.psum(partial_sum, ('col', 'depth'))]
    pallas_call x0 -> x1, Pallas kernels: none -> 50.9 us  [shards(): pl.pallas_call(functools.partial(kernel, rows, cols, depths), out_shape=j...]
    psum x2 -> x0, blocking collectives: 34.2 us -> none  [shards(): column_sum = lax.psum(partial_sum, 'row')]
    all_gather x2 -> x0, blocking collectives: 18.9 us -> none  [shards(): gathered = lax.all_gather(column_sum, ('col', 'depth'), axis=0, tiled=True)]
    dot_general x10 -> x0, matrix products: 18.4 us -> none  [the longest x3 8.07 us: apply_lower(): return jnp.einsum('pkij,pkrj->pri', diag_band, windows, precision=PREC)]
    ppermute x6 -> x0, waiting for transfers between devices: 17.7 us -> none  [from_behind(): return lax.ppermute(shard, axis, pairs)]
    ppermute x6 -> x0, starting transfers between devices: 15.6 us -> none  [from_behind(): return lax.ppermute(shard, axis, pairs)]
    unnamed x9 -> x12, local copies, waits for them, and re-layouts: 0.02 us -> 6.29 us
  transfers between devices with their start and end apart: 10 -> 0, of which waited for: 9 -> 0; matrix products, arithmetic and copies ran while one was open for 1% -> 0% of each run, Pallas kernels for 0% -> 0%
where the time goes in v1:
time: 57.5 us; the launch traced here: 57.2 us
  Pallas kernels  50.9 us (89%)
  local copies, waits for them, and re-layouts  6.29 us (11%)
    pallas_call x1, Pallas kernels, shards(): pl.pallas_call(functools.partial(kernel, rows, cols, depths), out_shape=j...  50.9 us
    unnamed x12, local copies, waits for them, and re-layouts  6.29 us

profile of v1, /device:TPU:0, one launch (start us, length us, event | category | flops | bytes accessed | tf_op | source)
XLA Modules:
  0.0 57.2 jit_solution(7275320144941370287)
XLA Ops:
  0.0 0.8 %copy.7.pattern_ref = s32[6,3]{1,0:T(8,128)S(1)} copy(s32[6,3]{0,1:T(4,128)} %param.8) | data formatting | bytes 144 | tf_op args[2]
  0.8 0.0 copy-start
  0.8 1.4 %copy-done = f32[6,4,128,128]{3,2,1,0:T(8,128)S(1)} copy-done((f32[6,4,128,128]{3,2,1,0:T(8,128)S(1)}, f32[6,4,128,128]{3,2,1,0:T(8,128)}, u32[]{:S(2)}) %copy-start) | copy-done | bytes 1572888
  2.2 0.0 copy-start.1
  2.2 1.3 %copy-done.1 = f32[6,3,128,128]{3,2,1,0:T(8,128)S(1)} copy-done((f32[6,3,128,128]{3,2,1,0:T(8,128)S(1)}, f32[6,3,128,128]{3,2,1,0:T(8,128)}, u32[]{:S(2)}) %copy-start.1) | copy-done | bytes 1179672
  3.4 0.0 copy-start.2
  3.4 0.9 %copy-done.2 = f32[6,32,128]{2,1,0:T(8,128)S(1)} copy-done((f32[6,32,128]{2,1,0:T(8,128)S(1)}, f32[6,32,128]{2,1,0:T(8,128)}, u32[]{:S(2)}) %copy-start.2) | copy-done | bytes 98328
  4.3 0.0 copy-start.3
  4.3 0.7 %copy-done.3 = s32[24]{0:T(128)S(1)} copy-done((s32[24]{0:T(128)S(1)}, s32[24]{0:T(128)}, u32[]{:S(2)}) %copy-start.3) | copy-done | bytes 120
  5.0 0.0 copy-start.4
  5.0 0.7 %copy-done.4 = s32[9]{0:T(128)S(1)} copy-done((s32[9]{0:T(128)S(1)}, s32[9]{0:T(128)}, u32[]{:S(2)}) %copy-start.4) | copy-done | bytes 60
  5.7 50.9 %shard_map.64 = f32[6,32,128]{2,1,0:T(8,128)S(1)} custom-call(f32[6,32,128]{2,1,0:T(8,128)S(1)} %copy-done.2, f32[6,3,128,128]{3,2,1,0:T(8,128)S(1)} %copy-done.1, s32[6,3]{1,0:T(8,128)S(1)} %copy.7.pattern_ref, f32[6,4,128,128]{3,2,1,0:T(8,128)S(1)} %copy-done, s32[24]{0:T(128)S(1)} %copy-done.3, s32[9]{0:T(128)S(1)} %copy-done.4), custom_call_target="tpu_custom_call" | custom-call | tf_op jit(solution)/shard_map/pallas_call | solution.py:406
  56.6 0.6 %copy.9 = f32[6,32,128]{2,1,0:T(8,128)} copy(f32[6,32,128]{2,1,0:T(8,128)S(1)} %shard_map.64) | data formatting | bytes 196608
Async XLA Ops:
  0.8 1.4 %copy-start = (f32[6,4,128,128]{3,2,1,0:T(8,128)S(1)}, f32[6,4,128,128]{3,2,1,0:T(8,128)}, u32[]{:S(2)}) copy-start(f32[6,4,128,128]{3,2,1,0:T(8,128)} %inverses_hbm.1) | copy-start | bytes 4718596
  2.2 1.3 %copy-start.1 = (f32[6,3,128,128]{3,2,1,0:T(8,128)S(1)}, f32[6,3,128,128]{3,2,1,0:T(8,128)}, u32[]{:S(2)}) copy-start(f32[6,3,128,128]{3,2,1,0:T(8,128)} %factor_hbm.1) | copy-start | bytes 3538948
  3.4 0.9 %copy-start.2 = (f32[6,32,128]{2,1,0:T(8,128)S(1)}, f32[6,32,128]{2,1,0:T(8,128)}, u32[]{:S(2)}) copy-start(f32[6,32,128]{2,1,0:T(8,128)} %rhs_ref.1) | copy-start | bytes 294916
  4.3 0.7 %copy-start.3 = (s32[24]{0:T(128)S(1)}, s32[24]{0:T(128)}, u32[]{:S(2)}) copy-start(s32[24]{0:T(128)} %supernodes_ref.1) | copy-start | bytes 292
  5.0 0.7 %copy-start.4 = (s32[9]{0:T(128)S(1)}, s32[9]{0:T(128)}, u32[]{:S(2)}) copy-start(s32[9]{0:T(128)} %levels_ref.1) | copy-start | bytes 112

commit v2 on v1

--- a/solution.py
+++ b/solution.py
@@ -28,9 +28,9 @@
 
 
 def kernel(
-    rows, cols, depths, rhs_ref, factor_hbm, pattern_ref, inverses_hbm, supernodes_ref, levels_ref,
+    rows, cols, depths, rhs_hbm, factor_hbm, pattern_hbm, inverses_hbm, supernodes_hbm, levels_hbm,
     out_ref,
-    factor_ref, inverses_ref, w_high, w_low, d_high, d_low,
+    rhs_ref, pattern_ref, supernodes_ref, levels_ref, factor_ref, inverses_ref, w_high, w_low, d_high, d_low,
     start_ref, wide_ref, pad_ref, solved_ref, answer_ref,
     send_d, recv_d, send_b, recv_b, send_e, recv_e, send_g, recv_g,
     load_sems, start_sems, d_sems, b_sems, e_sems, g_sems,
@@ -68,9 +68,24 @@
         inverses_hbm.at[pl.ds(depth * col_tiles, col_tiles)], inverses_ref, load_sems.at[0]
     )
     load_factor = pltpu.make_async_copy(factor_hbm, factor_ref, load_sems.at[1])
+    small_loads = [
+        pltpu.make_async_copy(src, dst, load_sems.at[2 + i])
+        for i, (src, dst) in enumerate(
+            [
+                (rhs_hbm, rhs_ref),
+                (supernodes_hbm, supernodes_ref),
+                (levels_hbm, levels_ref),
+                (pattern_hbm, pattern_ref),
+            ]
+        )
+    ]
+    for load in small_loads:
+        load.start()
     load_inverses.start()
     load_factor.start()
     lax.fori_loop(1, count, greet, 0, unroll=count <= 64)
+    for load in small_loads:
+        load.wait()
 
     def push(src, dst, sems, to):
         pltpu.make_async_remote_copy(
@@ -112,12 +127,6 @@
     @pl.when(lower & first)
     def _():
         start_ref[0] = jnp.zeros((chunk, span), F32)
-
-    pl.semaphore_wait(barrier, count - 1)
-
-    @pl.when(upper & jnp.logical_not(last))
-    def _():
-        push(start_ref.at[1], start_ref.at[0], start_sems, device(row + 1, col, 0))
 
     load_inverses.wait()
     own_first = row * row_tiles + depth * col_tiles
@@ -140,6 +149,26 @@
             d_high[t, :, k * width : (k + 1) * width] = high.astype(BF16)
             d_low[t, :, k * width : (k + 1) * width] = low.astype(BF16)
 
+    load_factor.wait()
+    row_level = [level_of(row * row_tiles + p) for p in range(row_tiles)]
+    col_level = [level_of(place * col_tiles + q) for q in range(col_tiles)]
+    for p in range(row_tiles):
+        for q in range(col_tiles):
+            keep = (row_level[p] > col_level[q]) & (pattern_ref[q, p] > 0)
+            high, low = halves(factor_ref[p, q] * jnp.where(keep, one, zero))
+            at = (slice(p * width, (p + 1) * width), slice(q * width, (q + 1) * width))
+            w_high[at] = high.astype(BF16)
+            w_low[at] = low.astype(BF16)
+    row_mask = [
+        lanes([jnp.where(v == level, one, zero) for v in row_level]) for level in range(LEVELS)
+    ]
+
+    pl.semaphore_wait(barrier, count - 1)
+
+    @pl.when(upper & jnp.logical_not(last))
+    def _():
+        push(start_ref.at[1], start_ref.at[0], start_sems, device(row + 1, col, 0))
+
     @pl.when(lower & jnp.logical_not(first))
     def _():
         pltpu.make_async_copy(start_ref.at[0], start_ref.at[0], start_sems.at[1]).wait()
@@ -186,20 +215,6 @@
 
     solve_own(0, start_vector())
     spread_solved(0)
-
-    load_factor.wait()
-    row_level = [level_of(row * row_tiles + p) for p in range(row_tiles)]
-    col_level = [level_of(place * col_tiles + q) for q in range(col_tiles)]
-    for p in range(row_tiles):
-        for q in range(col_tiles):
-            keep = (row_level[p] > col_level[q]) & (pattern_ref[p, q] > 0)
-            high, low = halves(factor_ref[p, q] * jnp.where(keep, one, zero))
-            at = (slice(p * width, (p + 1) * width), slice(q * width, (q + 1) * width))
-            w_high[at] = high.astype(BF16)
-            w_low[at] = low.astype(BF16)
-    row_mask = [
-        lanes([jnp.where(v == level, one, zero) for v in row_level]) for level in range(LEVELS)
-    ]
 
     column_cases = [(jnp.logical_not(home), rows), (home, rows - 1)]
 
@@ -399,16 +414,19 @@
     chunk, span = rhs // cols, col_tiles * width
     unit = (chunk, span)
     vmem = pl.BlockSpec(memory_space=pltpu.VMEM)
-    smem = pl.BlockSpec(memory_space=pltpu.SMEM)
-    hbm = pl.BlockSpec(memory_space=pl.ANY)
+    hbm = pl.BlockSpec(memory_space=pltpu.HBM)
     steps = LEVELS - 1
     dma = pltpu.SemaphoreType.DMA
     return pl.pallas_call(
         functools.partial(kernel, rows, cols, depths),
         out_shape=jax.ShapeDtypeStruct(right_sides.shape, F32),
-        in_specs=[vmem, hbm, smem, hbm, smem, smem],
+        in_specs=[hbm] * 6,
         out_specs=vmem,
         scratch_shapes=[
+            pltpu.VMEM(right_sides.shape, F32),
+            pltpu.SMEM(pattern.shape[::-1], jnp.int32),
+            pltpu.SMEM(supernodes.shape, jnp.int32),
+            pltpu.SMEM(levels.shape, jnp.int32),
             pltpu.VMEM(factor.shape, F32),
             pltpu.VMEM((col_tiles,) + inverses.shape[1:], F32),
             pltpu.VMEM((row_tiles * width, span), BF16),
@@ -428,7 +446,7 @@
             pltpu.VMEM((LEVELS, 4 * cols) + unit, F32),
             pltpu.VMEM((steps, cols) + unit, F32),
             pltpu.VMEM((steps, rows) + unit, F32),
-            dma((2,)),
+            dma((6,)),
             dma((2,)),
             dma((steps, 2)),
             dma((steps, 2)),
@@ -436,9 +454,9 @@
             dma((steps, 2)),
         ],
         compiler_params=pltpu.CompilerParams(
-            collective_id=0, has_side_effects=True, vmem_limit_bytes=32 * 1024 * 1024
+            collective_id=0, has_side_effects=True, vmem_limit_bytes=60 * 1024 * 1024
         ),
-    )(right_sides, factor, pattern, inverses, supernodes, levels)
+    )(right_sides, factor, pattern.T, inverses, supernodes, levels)
 
 
 def solution(mesh):

time: 57.5 us -> 52.3 us (0.910)
  local copies, waits for them, and re-layouts: 6.29 us -> 1.54 us
    unnamed x12 -> x1, local copies, waits for them, and re-layouts: 6.29 us -> 1.54 us
where the time goes in v2:
time: 52.3 us; the launch traced here: 52.2 us
  Pallas kernels  50.6 us (97%)
  local copies, waits for them, and re-layouts  1.54 us (3%)
    pallas_call x1, Pallas kernels, shards(): pl.pallas_call(functools.partial(kernel, rows, cols, depths), out_shape=j...  50.6 us
    unnamed x1, local copies, waits for them, and re-layouts  1.54 us

profile of v2, /device:TPU:0, one launch (start us, length us, event | category | flops | bytes accessed | tf_op | source)
XLA Modules:
  0.0 52.2 jit_solution(3858093465923393023)
XLA Ops:
  0.0 50.6 %shard_map.64 = f32[6,32,128]{2,1,0:T(8,128)} custom-call(f32[6,32,128]{2,1,0:T(8,128)} %rhs_hbm.1, f32[6,3,128,128]{3,2,1,0:T(8,128)} %factor_hbm.1, s32[3,6]{1,0:T(4,128)} %bitcast.1, f32[6,4,128,128]{3,2,1,0:T(8,128)} %inverses_hbm.1, s32[24]{0:T(128)} %supernodes_hbm.1, s32[9]{0:T(128)} %levels_hbm.1), custom_call_target="tpu_custom_call" | custom-call | tf_op jit(solution)/shard_map/pallas_call | solution.py:420
  50.6 1.5 %copy.8 = f32[6,32,128]{2,1,0:T(8,128)} copy(f32[6,32,128]{2,1,0:T(8,128)} %shard_map.64) | data formatting | bytes 196608
